TPU v7x, 512 devices: a whole 4x8x8 slice. The times are simulated.
512 devices in a mesh: group: 16 (over y, x_lo), fsdp: 32 (over x_hi, z, core).
Axes of the slice: x: 4 (x_hi: 2, x_lo: 2; x = x_hi * 2 + x_lo), y: 8, z: 8, core: 2. Of those that a mesh axis runs over, the one named last changes fastest.
Arguments:
- grad_terms: bfloat16 [16, 32, 64, 8192], P('group', 'fsdp'), may hold values from -0.59765625 to 0.59765625
- master: float32 [64, 8192], P('fsdp'), may hold values from -6 to 6
- inner_drift: float32 [16, 64, 8192], P('group', 'fsdp'), may hold values from -0.6 to 0.6
- momentum: float32 [64, 8192], P('fsdp'), may hold values from -3 to 3
- moment_codes: int32 [16, 64, 8192], P('group', 'fsdp'), may hold values from 0 to 255
- second_codes: int32 [16, 64, 8192], P('group', 'fsdp'), may hold values from 0 to 255
- moment_scale: float32 [16, 64, 32], P('group', 'fsdp'), may hold values from 0.01 to 0.1
- second_scale: float32 [16, 64, 32], P('group', 'fsdp'), may hold values from 0.05 to 0.5
- counts: int32 [16], P('group'), may hold values from 256 to 6144, as said below
Outputs:
- master_new: float32 [64, 8192], P('fsdp')
- momentum_new: float32 [64, 8192], P('fsdp')
- moment_new: float32 [16, 64, 8192], P('group', 'fsdp')
- second_new: float32 [16, 64, 8192], P('group', 'fsdp')
- model_copy: bfloat16 [64, 8192], replicated
Inputs may be any that keep to these rules, and one draw needn't show every extreme that they name: `counts`: one group trained on 6144 tokens, every other on 256 to 2048.
All inputs are finite; a program needn't handle non-finite values.
Results may differ from a plain program's by a relative error of at most 0.0004.
Values may be sent and summed in bfloat16 or wider, within the bound.
A program may use at most 64 MiB of HBM per device.

v0:
```python
import jax
import jax.numpy as jnp
from jax import lax
from jax.sharding import PartitionSpec as P

BLOCK = 256
STEP = 500


def blockwise(values, scale):
    shaped = values.reshape(values.shape[:-1] + (values.shape[-1] // BLOCK, BLOCK))
    return (shaped * scale[..., None]).reshape(values.shape)


def nesterov(mean_pseudo, master, momentum):
    momentum_new = 0.9 * momentum + mean_pseudo
    master_new = master - 0.7 * (mean_pseudo + 0.9 * momentum_new)
    return (master_new, momentum_new)


def on_device(
    grad_terms,
    master,
    inner_drift,
    momentum,
    moment_codes,
    second_codes,
    moment_scale,
    second_scale,
    counts,
):
    inner = master + inner_drift[0]
    weight = counts.astype(jnp.float32)[0]
    summed = lax.psum_scatter(
        grad_terms.astype(jnp.float32), "fsdp", scatter_dimension=2, tiled=True
    )
    grad = summed[:, 0]
    signed = (moment_codes.astype(jnp.float32) - 127.5) / 127.5
    moment_old = blockwise(signed * signed * signed, moment_scale)
    unsigned = (second_codes.astype(jnp.float32) + 16.0) / 271.0
    second_old = blockwise(unsigned * unsigned, second_scale)
    moment_new = 0.9 * moment_old + 0.1 * grad
    second_new = 0.999 * second_old + 0.001 * grad * grad
    update = moment_new / (1.0 - 0.9**STEP) / (jnp.sqrt(second_new / (1.0 - 0.999**STEP)) + 1e-08)
    pseudo = master - (inner - 0.8 * (update[0] + 0.025 * inner))
    weighted = weight * pseudo
    total_rows, total_count = lax.psum((weighted, weight), "group")
    master_new, momentum_new = nesterov(total_rows / total_count, master, momentum)
    model_copy = lax.all_gather(master_new.astype(jnp.bfloat16), "fsdp", axis=0, tiled=True)
    return (master_new, momentum_new, moment_new, second_new, model_copy)


def solution(mesh):
    in_specs = (
        P("group", "fsdp", None, None),
        P("fsdp", None),
        P("group", "fsdp", None),
        P("fsdp", None),
        P("group", "fsdp", None),
        P("group", "fsdp", None),
        P("group", "fsdp", None),
        P("group", "fsdp", None),
        P("group"),
    )
    out_specs = (
        P("fsdp", None),
        P("fsdp", None),
        P("group", "fsdp", None),
        P("group", "fsdp", None),
        P(),
    )
    return jax.shard_map(
        on_device, mesh=mesh, in_specs=in_specs, out_specs=out_specs, check_vma=False
    )
```

profile of v0, /device:TPU:1, one launch (start us, length us, event | category | flops | bytes accessed | tf_op | source)
XLA Modules:
  0.0 398.8 jit_solution(11685884509597873997)
XLA Ops:
  7.2 0.0 copy-start.5
  7.2 0.0 copy-start.6
  7.2 0.0 copy-start
  7.2 0.0 copy-start.1
  7.2 0.0 copy-start.3
  7.2 0.0 copy-start.2
  7.2 0.0 all-reduce.4.cloned.1.call-start
  8.0 0.0 copy-start.4
  8.0 157.2 %all-reduce.5 = f32[1,1,64,8192]{3,2,1,0:T(8,128)S(1)} all-reduce(bf16[1,1,64,8192]{3,2,1,0:T(8,128)(2,1)} %param.9), channel_id=2, replica_groups=mesh['group'=16,'fsdp'=32] {'fsdp'}, use_global_device_ids=true, to_apply=%region_0.0.clone | all-reduce | flops 524288 | bytes 3145728
  165.1 0.0 copy-done.5
  165.2 0.1 mul.137
  165.3 0.0 copy-done.6
  165.3 0.1 mul.146
  165.4 1.3 dynamic-slice
  167.3 0.0 copy-done
  167.4 0.0 copy-done.1
  167.4 0.0 copy-done.3
  167.4 0.0 copy-done.2
  167.4 1.0 fusion.7
  168.4 0.0 all-reduce.4.cloned.1.call-update
  168.4 0.0 all-gather.3.cloned.1.call-start
  168.5 28.3 %psum.15 = f32[]{:T(128)} all-reduce(f32[]{:T(128)} %bitcast.2), channel_id=1, replica_groups=mesh['group'=16,'fsdp'=32] {'group'}, use_global_device_ids=true, to_apply=%region_2.0 | all-reduce | flops 1 | bytes 8 | tf_op jit(solution)/shard_map/psum | solution.py:47
  196.8 95.9 %all-reduce.4.cloned.1.call-done = f32[2,8192]{1,0:T(2,128)} async-done(((f32[2,8192]{1,0:T(2,128)}), f32[2,8192]{1,0:T(2,128)}) %all-reduce.4.cloned.1.call-update) | async-done | bytes 65552 | tf_op jit(solution)/shard_map/psum | solution.py:47
  292.7 0.0 copy-done.4
  292.7 2.2 convert_bitcast_fusion
  294.9 0.0 all-gather.3.cloned.1.call-update
  295.0 94.7 %all-gather.3.cloned.1.call-done = bf16[32,2,8192]{2,1,0:T(2,128)(2,1)} async-done(((bf16[1,2,8192]{2,1,0:T(2,128)(2,1)}), bf16[32,2,8192]{2,1,0:T(2,128)(2,1)}) %all-gather.3.cloned.1.call-update) | async-done | bytes 1048592 | tf_op jit(solution)/shard_map/all_gather | solution.py:49
  389.7 2.2 reshape.84
  (2 shorter events, 0.1 us)
Async XLA Ops:
  7.2 158.0 %copy-start.5 = (f32[1,2,32]{2,1,0:T(2,128)S(1)}, f32[1,2,32]{2,1,0:T(2,128)}, u32[]{:S(2)}) copy-start(f32[1,2,32]{2,1,0:T(2,128)} %param.15) | copy-start | bytes 772
  7.2 158.1 %copy-start.6 = (f32[1,2,32]{2,1,0:T(2,128)S(1)}, f32[1,2,32]{2,1,0:T(2,128)}, u32[]{:S(2)}) copy-start(f32[1,2,32]{2,1,0:T(2,128)} %param.16) | copy-start | bytes 772
  7.2 160.2 %copy-start = (f32[2,8192]{1,0:T(2,128)S(1)}, f32[2,8192]{1,0:T(2,128)}, u32[]{:S(2)}) copy-start(f32[2,8192]{1,0:T(2,128)} %param.10) | copy-start | bytes 196612
  7.2 160.2 %copy-start.1 = (f32[1,2,8192]{2,1,0:T(2,128)S(1)}, f32[1,2,8192]{2,1,0:T(2,128)}, u32[]{:S(2)}) copy-start(f32[1,2,8192]{2,1,0:T(2,128)} %param.11) | copy-start | bytes 196612
  7.2 160.2 %copy-start.3 = (s32[1,2,8192]{2,1,0:T(2,128)S(1)}, s32[1,2,8192]{2,1,0:T(2,128)}, u32[]{:S(2)}) copy-start(s32[1,2,8192]{2,1,0:T(2,128)} %param.13) | copy-start | bytes 196612
  7.2 160.2 %copy-start.2 = (s32[1,2,8192]{2,1,0:T(2,128)S(1)}, s32[1,2,8192]{2,1,0:T(2,128)}, u32[]{:S(2)}) copy-start(s32[1,2,8192]{2,1,0:T(2,128)} %param.14) | copy-start | bytes 196612
  7.2 285.5 %all-reduce.4.cloned.1.call-start = ((), (), s32[]{:S(2)}) async-start(), calls=%async_computation | async-start | bytes 131072 | tf_op jit(solution)/shard_map/psum | solution.py:47
  8.0 284.7 %copy-start.4 = (f32[2,8192]{1,0:T(2,128)S(1)}, f32[2,8192]{1,0:T(2,128)}, u32[]{:S(2)}) copy-start(f32[2,8192]{1,0:T(2,128)} %param.12) | copy-start | bytes 196612
  168.4 221.3 %all-gather.3.cloned.1.call-start = ((), (), s32[]{:S(2)}) async-start(), calls=%async_computation.1 | async-start | bytes 1081344 | tf_op jit(solution)/shard_map/all_gather | solution.py:49
Sparse Core Ops, SparseCore 0:
  168.5 124.1 all-reduce.3
  297.2 92.4 all-gather.2
where the time goes:
time: 399 us
  waiting for transfers between devices  191 us (48%)
  blocking collectives  185 us (46%)
  between operations  15.5 us (4%)
    unnamed x1, blocking collectives  157 us
    psum x1, waiting for transfers between devices, on_device(): total_rows, total_count = lax.psum((weighted, weight), 'group')  95.9 us
    all_gather x1, waiting for transfers between devices, on_device(): lax.all_gather(master_new.astype(jnp.bfloat16), 'fsdp', axis=0, tiled=True)  94.7 us
    psum x1, blocking collectives, on_device(): total_rows, total_count = lax.psum((weighted, weight), 'group')  28.3 us
  transfers between devices with their start and end apart: 2, of which 2 were waited for; matrix products, arithmetic and copies ran while one was open for 0% of the time, Pallas kernels for 0%

commit v1 on v0

--- a/solution.py
+++ b/solution.py
@@ -46,7 +46,9 @@
     weighted = weight * pseudo
     total_rows, total_count = lax.psum((weighted, weight), "group")
     master_new, momentum_new = nesterov(total_rows / total_count, master, momentum)
-    model_copy = lax.all_gather(master_new.astype(jnp.bfloat16), "fsdp", axis=0, tiled=True)
+    x = master_new.astype(jnp.bfloat16)
+    sent = jnp.stack([x] * lax.axis_size("fsdp"))
+    model_copy = jnp.concatenate(lax.all_to_all(sent, "fsdp", 0, 0), axis=0)
     return (master_new, momentum_new, moment_new, second_new, model_copy)
 
 

time: 399 us -> 354 us (0.89)
  waiting for transfers between devices: 191 us -> 96 us
  blocking collectives: 185 us -> 234 us
    all_gather x1 -> x0, waiting for transfers between devices: 94.7 us -> none  [on_device(): lax.all_gather(master_new.astype(jnp.bfloat16), 'fsdp', axis=0, tiled=True)]
    all_to_all x0 -> x1, blocking collectives: none -> 48.5 us  [on_device(): model_copy = jnp.concatenate(lax.all_to_all(sent, 'fsdp', 0, 0), axis=0)]
  transfers between devices with their start and end apart: 2 -> 1, of which waited for: 2 -> 1; matrix products, arithmetic and copies ran while one was open for 0% -> 0% of each run, Pallas kernels for 0% -> 0%
where the time goes in v1:
time: 354 us; the launch traced here: 352 us
  blocking collectives  234 us (66%)
  waiting for transfers between devices  96 us (27%)
  between operations  15.5 us (4%)
  local copies, waits for them, and re-layouts  3.66 us (1%)
    unnamed x1, blocking collectives  157 us
    psum x1, waiting for transfers between devices, on_device(): total_rows, total_count = lax.psum((weighted, weight), 'group')  96 us
    all_to_all x1, blocking collectives, on_device(): model_copy = jnp.concatenate(lax.all_to_all(sent, 'fsdp', 0, 0), axis=0)  48.5 us
    psum x1, blocking collectives, on_device(): total_rows, total_count = lax.psum((weighted, weight), 'group')  28.3 us
  transfers between devices with their start and end apart: 1, of which 1 were waited for; matrix products, arithmetic and copies ran while one was open for 0% of the time, Pallas kernels for 0%

profile of v1, /device:TPU:1, one launch (start us, length us, event | category | flops | bytes accessed | tf_op | source)
XLA Modules:
  0.0 352.4 jit_solution(10713294034037916916)
XLA Ops:
  7.2 0.0 copy-start.5
  7.2 0.0 copy-start.6
  7.2 0.0 copy-start
  7.2 0.0 copy-start.1
  7.2 0.0 copy-start.3
  7.2 0.0 copy-start.2
  7.2 0.0 all-reduce.4.cloned.1.call-start
  8.0 0.0 copy-start.4
  8.0 157.2 %all-reduce.5 = f32[1,1,64,8192]{3,2,1,0:T(8,128)S(1)} all-reduce(bf16[1,1,64,8192]{3,2,1,0:T(8,128)(2,1)} %param.9), channel_id=2, replica_groups=mesh['group'=16,'fsdp'=32] {'fsdp'}, use_global_device_ids=true, to_apply=%region_0.0.clone | all-reduce | flops 524288 | bytes 3145728
  165.1 0.0 copy-done.5
  165.2 0.1 mul.137
  165.3 0.0 copy-done.6
  165.3 0.1 mul.146
  165.4 1.3 dynamic-slice
  167.3 0.0 copy-done
  167.4 0.0 copy-done.1
  167.4 0.0 copy-done.3
  167.4 0.0 copy-done.2
  167.4 1.0 fusion.7
  168.4 0.0 all-reduce.4.cloned.1.call-update
  168.4 28.3 %psum.15 = f32[]{:T(128)} all-reduce(f32[]{:T(128)} %bitcast.2), channel_id=1, replica_groups=mesh['group'=16,'fsdp'=32] {'group'}, use_global_device_ids=true, to_apply=%region_2.0 | all-reduce | flops 1 | bytes 8 | tf_op jit(solution)/shard_map/psum | solution.py:47
  196.7 96.0 %all-reduce.4.cloned.1.call-done = f32[2,8192]{1,0:T(2,128)} async-done(((f32[2,8192]{1,0:T(2,128)}), f32[2,8192]{1,0:T(2,128)}) %all-reduce.4.cloned.1.call-update) | async-done | bytes 65552 | tf_op jit(solution)/shard_map/psum | solution.py:47
  292.7 0.0 copy-done.4
  292.7 2.2 fusion.8
  295.0 0.9 stack.2
  295.9 48.5 %all_to_all.5 = bf16[32,2,8192]{2,1,0:T(2,128)(2,1)S(1)} all-to-all(bf16[32,2,8192]{2,1,0:T(2,128)(2,1)S(1)} %stack.2), channel_id=1, replica_groups=mesh['group'=16,'fsdp'=32] {'fsdp'}, dimensions={0} | all-to-all | bytes 2097152 | tf_op jit(solution)/shard_map/all_to_all | solution.py:51
  344.4 1.2 reshape.88
  (2 shorter events, 0.1 us)
Async XLA Ops:
  7.2 158.0 %copy-start.5 = (f32[1,2,32]{2,1,0:T(2,128)S(1)}, f32[1,2,32]{2,1,0:T(2,128)}, u32[]{:S(2)}) copy-start(f32[1,2,32]{2,1,0:T(2,128)} %param.15) | copy-start | bytes 772
  7.2 158.1 %copy-start.6 = (f32[1,2,32]{2,1,0:T(2,128)S(1)}, f32[1,2,32]{2,1,0:T(2,128)}, u32[]{:S(2)}) copy-start(f32[1,2,32]{2,1,0:T(2,128)} %param.16) | copy-start | bytes 772
  7.2 160.2 %copy-start = (f32[2,8192]{1,0:T(2,128)S(1)}, f32[2,8192]{1,0:T(2,128)}, u32[]{:S(2)}) copy-start(f32[2,8192]{1,0:T(2,128)} %param.10) | copy-start | bytes 196612
  7.2 160.2 %copy-start.1 = (f32[1,2,8192]{2,1,0:T(2,128)S(1)}, f32[1,2,8192]{2,1,0:T(2,128)}, u32[]{:S(2)}) copy-start(f32[1,2,8192]{2,1,0:T(2,128)} %param.11) | copy-start | bytes 196612
  7.2 160.2 %copy-start.3 = (s32[1,2,8192]{2,1,0:T(2,128)S(1)}, s32[1,2,8192]{2,1,0:T(2,128)}, u32[]{:S(2)}) copy-start(s32[1,2,8192]{2,1,0:T(2,128)} %param.13) | copy-start | bytes 196612
  7.2 160.2 %copy-start.2 = (s32[1,2,8192]{2,1,0:T(2,128)S(1)}, s32[1,2,8192]{2,1,0:T(2,128)}, u32[]{:S(2)}) copy-start(s32[1,2,8192]{2,1,0:T(2,128)} %param.14) | copy-start | bytes 196612
  7.2 285.5 %all-reduce.4.cloned.1.call-start = ((), (), s32[]{:S(2)}) async-start(), calls=%async_computation.1 | async-start | bytes 131072 | tf_op jit(solution)/shard_map/psum | solution.py:47
  8.0 284.7 %copy-start.4 = (f32[2,8192]{1,0:T(2,128)S(1)}, f32[2,8192]{1,0:T(2,128)}, u32[]{:S(2)}) copy-start(f32[2,8192]{1,0:T(2,128)} %param.12) | copy-start | bytes 196612
Sparse Core Ops, SparseCore 0:
  168.5 124.1 all-reduce.3
